TPU v7x, 512 devices: a whole 4x4x16 slice. The times are simulated.
512 devices in a mesh: lat: 16 (over x_hi, y, core), lon: 32 (over z, x_lo).
Axes of the slice: x: 4 (x_hi: 2, x_lo: 2; x = x_hi * 2 + x_lo), y: 4, z: 16, core: 2. Of those that a mesh axis runs over, the one named last changes fastest.
Arguments:
- tokens: bfloat16 [2, 192, 384, 1024], P(None, 'lat', 'lon'), may hold values from -96 to 96
- qkv_weight: bfloat16 [1024, 1536], P('lon'), may hold values from -0.1875 to 0.1875
- out_weight: bfloat16 [512, 1024], P('lon'), may hold values from -1 to 1
- norm_gain: float32 [1024], replicated, may hold values from 0.1 to 1.9
- norm_bias: float32 [1024], replicated, may hold values from -3 to 3
- mixed_grad: bfloat16 [2, 192, 384, 1024], P(None, 'lat', 'lon'), may hold values from -6 to 6
Outputs:
- mixed: bfloat16 [2, 192, 384, 1024], P(None, 'lat', 'lon')
- token_grad: bfloat16 [2, 192, 384, 1024], P(None, 'lat', 'lon')
All inputs are finite; a program needn't handle non-finite values.
Results may differ from a plain program's by a relative error of at most 0.014.
The roundings to bfloat16 on the way count: a program that leaves them out, or rounds other values in their place, can miss the bound.
Values may be sent and summed in bfloat16 or wider, within the bound.
A program may use at most 64 MiB of HBM per device.

v0:
```python
import functools

import jax
import jax.numpy as jnp
from jax import lax
from jax.experimental import pallas as pl
from jax.experimental.pallas import tpu as pltpu
from jax.sharding import PartitionSpec as P

MESH = pl.DeviceIdType.MESH
BF = jnp.bfloat16
F32 = jnp.float32

D = 1024
HEADS = 8
HEAD_DIM = 64
LEV = 2
WIN = 12
INNER = 512
HALF = 6
TOK = LEV * WIN * WIN
QUARTER = TOK // 4
GROUP = 4
GW = GROUP * HEAD_DIM
WIDE = GROUP * TOK
ROWS = 32
EPS = 1e-05

HALVES = ((1, 1), (1, 0), (0, 1), (0, 0))


def nt(a, b):
    return lax.dot_general(a, b, (((1,), (1,)), ((), ())), preferred_element_type=F32)


def nn(a, b):
    return lax.dot_general(a, b, (((1,), (0,)), ((), ())), preferred_element_type=F32)


def tn(a, b):
    return lax.dot_general(a, b, (((0,), (0,)), ((), ())), preferred_element_type=F32)


def ds(start, size):
    return pl.ds(pl.multiple_of(start, size), size)


def kernel(
    n_lat, n_lon,
    t_ref, g_ref, wq_ref, wo_ref, gain_hbm, bias_hbm,
    m_out, d_out,
    comb_q, comb_o, wqf, wof, gain_ref, bias_ref, land_t, land_g, xw, gw, packed, heads, attn, agrad, hgrad, pgrad,
    scores, pt, dst, qblk, doblk, wide, mixed, tgrad,
    own_sem, zs, zr, ys, yr, xs, xr, ss, sr, hs, hr,
):
    lat, lon = lax.axis_index("lat"), lax.axis_index("lon")
    nz, ny = n_lon // 2, n_lat // 4
    rq, ro = D // n_lon, INNER // n_lon
    core, par, z = lax.rem(lat, 2), lax.rem(lon, 2), lon // 2
    half, y = lat // (2 * ny), lax.rem(lat // 2, ny)
    lat_lo, lat_hi = lax.rem(lat + n_lat - 1, n_lat), lax.rem(lat + 1, n_lat)
    lon_lo, lon_hi = lax.rem(lon + n_lon - 1, n_lon), lax.rem(lon + 1, n_lon)
    sib = (lat + 1 - 2 * core, lon)
    differ = lax.rem(par + core, 2)
    across = lon + 1 - 2 * par
    x_to = (lax.rem(lat + differ * (n_lat // 2), n_lat), across)
    x_from = (lax.rem(lat + (1 - differ) * (n_lat // 2), n_lat), across)
    west, north, diag = (lat, lon_lo), (lat_lo, lon), (lat_lo, lon_lo)
    east, south, far = (lat, lon_hi), (lat_hi, lon), (lat_hi, lon_hi)

    def offset(yy, e):
        far_pair = e // 2
        size = (1 - far_pair) * (yy + 1) + far_pair * (2 * ny - yy)
        return (1 - 2 * lax.rem(e, 2)) * size

    def z_to(e):
        return (lat, 2 * lax.rem(z + offset(y, e) + nz, nz) + par)

    def source(yy, e):
        return lax.rem(z - offset(yy, e) + nz, nz)

    def y_to(way):
        return ((half * ny + lax.rem(y + 1 - 2 * way + ny, ny)) * 2 + core, lon)

    opposite = ((half * ny + lax.rem(y + 2, ny)) * 2 + core, lon)

    def line(group, c):
        return lax.rem(y + ny + (0, 2 * c - 1, 1 - 2 * c, 2)[group], ny)

    comb, cut = (comb_q, comb_o), (3 * INNER // 2, D // 2)
    own = [
        ((wq_ref, wo_ref)[b].at[:, c * cut[b] : (c + 1) * cut[b]], comb[b].at[c, par, 0])
        for b in range(2) for c in range(2)
    ]
    own = [pltpu.make_async_copy(src, to, own_sem.at[8 + k]) for k, (src, to) in enumerate(own)]
    for copy in own:
        copy.start()

    barrier = pltpu.get_barrier_semaphore()
    met = [z_to(e) for e in range(4)]
    met += [y_to(0), y_to(1), opposite, sib, x_to, x_from, west, north, diag, east, south, far]
    for who in met:
        pl.semaphore_signal(barrier, inc=1, device_id=who, device_id_type=MESH)
    for copy in own:
        copy.wait()
    pl.semaphore_wait(barrier, len(met))

    def remote(src, dst, send, recv, who):
        return pltpu.make_async_remote_copy(
            src_ref=src, dst_ref=dst, send_sem=send, recv_sem=recv, device_id=who, device_id_type=MESH
        )

    def quarter(ref, k):
        i, j = HALVES[k]
        return ref.at[pl.ds(i * HALF, HALF), pl.ds(j * HALF, HALF)]

    def halo_in(field, src, land):
        copies = [
            remote(quarter(src, k), land.at[k], hs.at[field * 4 + k], hr.at[field * 4 + k], who)
            for k, who in ((1, west), (2, north), (3, diag))
        ]
        return copies, pltpu.make_async_copy(quarter(src, 0), land.at[0], own_sem.at[4 + field])

    in_t = halo_in(0, t_ref, land_t)
    in_g = halo_in(1, g_ref, land_g)
    def slots(wave, group, count=1):
        if wave < 2:
            return pl.ds(1 + wave * 8 + group * 2, count * 2)
        return pl.ds(1 + group * 4, count * 4)

    def z_copy(b, e):
        slot = 1 + e if b else 1 + e // 2 * 8 + e % 2
        i = b * 4 + e
        return remote(comb[b].at[core, par, 0], comb[b].at[core, par, slot], zs.at[i], zr.at[i], z_to(e))

    def y_copy(wave, k):
        i, buf = wave * 3 + k, comb[wave // 2]
        return remote(
            buf.at[core, par, slots(wave, 0)], buf.at[core, par, slots(wave, k + 1)], ys.at[i], yr.at[i],
            (y_to(core), y_to(1 - core), opposite)[k],
        )

    def x_copy(wave, k, p):
        ref = comb[wave // 2].at[core, p, slots(wave, k, 1 + 2 * k)]
        i = wave * 2 + k
        return remote(ref, ref, xs.at[i], xr.at[i], x_to)

    def x_own(b, p):
        ref = comb[b].at[core, p, 0]
        return remote(ref, ref, xs.at[6 + b], xr.at[6 + b], x_to)

    def s_copy(wave, other, c):
        ref = comb[wave // 2].at[c, lax.rem(par + other, 2), slots(wave, 0, 4)]
        i = wave * 2 + other
        return remote(ref, ref, ss.at[i], sr.at[i], sib)

    def s_own(b, c):
        ref = comb[b].at[c, 1 - par, 0]
        return remote(ref, ref, ss.at[6 + b], sr.at[6 + b], sib)

    def place(wave):
        b = wave // 2
        full, size = ((wqf, rq), (wof, ro))[b]
        for c in range(2):
            found = [] if wave == 1 else [(0, z)]
            for j in range(4):
                for i in range(4 if b else 2):
                    e = i if b else 2 * wave + i
                    found.append((slots(wave, j).start + i, source(line(j, c), e)))
            for slot, zq in found:
                for p in range(2):
                    full[ds((zq * 2 + p) * size, size), c * cut[b] : (c + 1) * cut[b]] = comb[b][c, p, slot]

    local = [
        pltpu.make_async_copy(gain_hbm, gain_ref, own_sem.at[2]),
        pltpu.make_async_copy(bias_hbm, bias_ref, own_sem.at[3]),
        in_t[1],
        in_g[1],
    ]

    def rows_of(land, field):
        def step(t, carry):
            k, i = 2 * (t // 3), 2 * lax.rem(t, 3)
            two = [land[k + n, pl.ds(i, 2)].reshape(24, D) for n in (0, 1)]
            field[ds(t * 48, 48), :] = jnp.concatenate(two, axis=0)
            return carry

        lax.fori_loop(0, 6, step, 0)

    z_copies = [[z_copy(b, e) for e in range(4)] for b in range(2)]
    for copy in z_copies[0]:
        copy.start()
    x_own(0, par).start()
    for copy in local:
        copy.start()

    def from_z(wave):
        b = wave // 2
        for copy in z_copies[1] if b else z_copies[0][2 * wave : 2 * wave + 2]:
            copy.wait_recv()
        for k in (2, 0, 1):
            y_copy(wave, k).start()
        x_copy(wave, 0, par).start()
        if wave == 0:
            for copy in in_t[0]:
                copy.start()
        if wave == 1:
            for copy in z_copies[1]:
                copy.start()
            x_own(1, par).start()

    def from_y(wave):
        for k in range(3):
            y_copy(wave, k).wait_recv()
        x_copy(wave, 1, par).start()
        s_copy(wave, 0, core).start()

    def from_x(wave):
        if wave != 1:
            x_own(wave // 2, 1 - par).wait_recv()
            s_own(wave // 2, core).start()
        for k in range(2):
            x_copy(wave, k, 1 - par).wait_recv()
        s_copy(wave, 1, core).start()

    def from_s(wave):
        if wave != 1:
            s_own(wave // 2, 1 - core).wait_recv()
        for other in range(2):
            s_copy(wave, other, 1 - core).wait_recv()
        place(wave)

    from_z(0)
    from_y(0)
    from_z(1)
    from_x(0)
    from_y(1)
    for copy in in_t[0]:
        copy.wait_recv()
    for copy in local:
        copy.wait()
    rows_of(land_t, xw)
    from_s(0)
    from_x(1)
    from_z(2)
    for copy in in_g[0]:
        copy.start()
    from_s(1)
    from_y(2)

    for n in range(3 * INNER // 256):
        cols = slice(n * 256, n * 256 + 256)
        packed[:, cols] = nn(xw[...], wqf[:, cols]).astype(BF)

    lane_head = lax.broadcasted_iota(jnp.int32, (TOK, GW), 1) // HEAD_DIM
    banned = jnp.where(lat == n_lat - 1, -1e30, 0.0).astype(F32)

    def spread(rows):
        return [rows * (lane_head[0:1] == h).astype(F32).astype(BF) for h in range(GROUP)]

    def columns(g):
        return [ds(n * INNER + g * GW, GW) for n in range(3)]

    def turned(block):
        return block.astype(F32).T.astype(BF)

    def narrow(right, left):
        for c in range(0, WIDE, 384):
            wide[:, c : c + 384] = nn(right, left(slice(c, c + 384)))
        blocks = [wide[h * HEAD_DIM : (h + 1) * HEAD_DIM, h * TOK : (h + 1) * TOK] for h in range(GROUP)]
        return jnp.concatenate(blocks, axis=0).T.astype(BF)

    def forward(g, carry):
        q_at, k_at, v_at = columns(g)
        for h, rows in enumerate(spread(packed[:, q_at])):
            qblk[g, h * TOK : (h + 1) * TOK, :] = rows

        for c in range(0, WIDE, 384):
            scores[:, c : c + 384] = nt(packed[:, k_at], qblk[g, c : c + 384, :])
        for c in range(0, WIDE, 128):
            cols = slice(c, c + 128)
            query = lax.rem(c + lax.broadcasted_iota(jnp.int32, (1, 128), 1), TOK)
            side = (query >= TOK // 2).astype(F32)
            s = jnp.concatenate(
                [scores[: TOK // 2, cols] + side * banned, scores[TOK // 2 :, cols] + (1.0 - side) * banned], axis=0
            )
            top = jnp.max(s, axis=0, keepdims=True)
            e = jnp.exp((s - top) * (HEAD_DIM ** -0.5))
            pt[g, :, cols] = (e * (1.0 / jnp.sum(e, axis=0, keepdims=True))).astype(BF)
        heads[:, q_at] = narrow(turned(packed[:, v_at]), lambda cols: pt[g, :, cols])

        @pl.when(g == 0)
        def _():
            from_x(2)

        return carry

    lax.fori_loop(0, HEADS // GROUP, forward, 0)
    from_s(2)

    for n in range(0, D, 256):
        attn[:, n : n + 256] = nn(heads[...], wof[:, n : n + 256]).astype(BF)

    for copy in in_g[0]:
        copy.wait_recv()
    rows_of(land_g, gw)

    def norm(c, carry):
        rows = ds(c * ROWS, ROWS)
        a = attn[rows, :].astype(F32)
        gain = gain_ref[...]
        scaled = gw[rows, :].astype(F32) * gain
        centered = a - jnp.mean(a, axis=-1, keepdims=True)
        level = scaled - jnp.mean(scaled, axis=-1, keepdims=True)
        inverse = lax.rsqrt(jnp.mean(centered * centered, axis=-1, keepdims=True) + EPS)
        along = jnp.mean(scaled * centered, axis=-1, keepdims=True) * inverse
        normed = centered * inverse
        mixed[rows, :] = (xw[rows, :].astype(F32) + normed * gain + bias_ref[...]).astype(BF)
        agrad[rows, :] = ((level - normed * along) * inverse).astype(BF)
        return carry

    lax.fori_loop(0, TOK // ROWS, norm, 0, unroll=3)

    def halo_out(field, rows, land, out):
        def step(t, carry):
            k, i = 2 * (t // 3), 2 * lax.rem(t, 3)
            block = rows[ds(t * 48, 48), :]
            for n in (0, 1):
                land[k + n, pl.ds(i, 2)] = block[n * 24 : (n + 1) * 24].reshape(2, HALF, LEV, D)
            return carry

        lax.fori_loop(0, 6, step, 0)
        copies = [
            remote(land.at[k], quarter(out, k), hs.at[(field + 2) * 4 + k], hr.at[(field + 2) * 4 + k], who)
            for k, who in ((1, east), (2, south), (3, far))
        ]
        keep = pltpu.make_async_copy(land.at[0], quarter(out, 0), own_sem.at[6 + field])
        for copy in copies:
            copy.start()
        keep.start()
        return copies, keep

    out_m = halo_out(0, mixed, land_t, m_out)

    for n in range(0, INNER, 256):
        hgrad[:, n : n + 256] = nt(agrad[...], wof[n : n + 256, :]).astype(BF)

    def backward(g, carry):
        q_at, k_at, v_at = columns(g)
        for h, rows in enumerate(spread(hgrad[:, q_at])):
            doblk[h * TOK : (h + 1) * TOK, :] = rows

        for c in range(0, WIDE, 384):
            scores[:, c : c + 384] = nt(packed[:, v_at], doblk[c : c + 384, :])
        for c in range(0, WIDE, 128):
            cols = slice(c, c + 128)
            p, dp = pt[g, :, cols].astype(F32), scores[:, cols]
            total = jnp.sum(p * dp, axis=0, keepdims=True)
            dst[:, cols] = (p * (dp - total) * (HEAD_DIM ** -0.5)).astype(BF)
        pgrad[:, q_at] = narrow(turned(packed[:, k_at]), lambda cols: dst[:, cols])
        pgrad[:, v_at] = nn(pt[g], doblk[...]).astype(BF)
        pgrad[:, k_at] = nn(dst[...], qblk[g]).astype(BF)
        return carry

    lax.fori_loop(0, HEADS // GROUP, backward, 0)

    for n in range(0, D, 256):
        cols = slice(n, n + 256)
        sg = nt(pgrad[...], wqf[cols, :]).astype(BF).astype(F32)
        tgrad[:, cols] = (gw[:, cols].astype(F32) + sg).astype(BF)
    out_d = halo_out(1, tgrad, land_g, d_out)

    for copy in z_copies[0] + z_copies[1]:
        copy.wait_send()
    for wave in range(3):
        for k in range(3):
            y_copy(wave, k).wait_send()
        for k in range(2):
            x_copy(wave, k, par).wait_send()
            s_copy(wave, k, core).wait_send()
    for b in range(2):
        x_own(b, par).wait_send()
        s_own(b, core).wait_send()
    for copy in in_t[0] + in_g[0]:
        copy.wait_send()
    for copies, keep in (out_m, out_d):
        keep.wait()
        for copy in copies:
            copy.wait()


def per_device(n_lat, n_lon, tokens, qkv_weight, out_weight, norm_gain, norm_bias, mixed_grad):
    hbm = pl.BlockSpec(memory_space=pltpu.HBM)
    cells = (WIN, WIN, LEV, D)
    m_out, d_out = pl.pallas_call(
        functools.partial(kernel, n_lat, n_lon),
        out_shape=[jax.ShapeDtypeStruct(cells, BF)] * 2,
        in_specs=[hbm] * 6,
        out_specs=[pl.BlockSpec(memory_space=pl.ANY)] * 2,
        scratch_shapes=[
            pltpu.VMEM((2, 2, 17, D // n_lon, 3 * INNER // 2), BF),
            pltpu.VMEM((2, 2, 17, INNER // n_lon, D // 2), BF),
            pltpu.VMEM((D, 3 * INNER), BF),
            pltpu.VMEM((INNER, D), BF),
            pltpu.VMEM((1, D), F32),
            pltpu.VMEM((1, D), F32),
            pltpu.VMEM((4, HALF, HALF, LEV, D), BF),
            pltpu.VMEM((4, HALF, HALF, LEV, D), BF),
            pltpu.VMEM((TOK, D), BF),
            pltpu.VMEM((TOK, D), BF),
            pltpu.VMEM((TOK, 3 * INNER), BF),
            pltpu.VMEM((TOK, INNER), BF),
            pltpu.VMEM((TOK, D), BF),
            pltpu.VMEM((TOK, D), BF),
            pltpu.VMEM((TOK, INNER), BF),
            pltpu.VMEM((TOK, 3 * INNER), BF),
            pltpu.VMEM((TOK, WIDE), F32),
            pltpu.VMEM((2, TOK, WIDE), BF),
            pltpu.VMEM((TOK, WIDE), BF),
            pltpu.VMEM((2, WIDE, GW), BF),
            pltpu.VMEM((WIDE, GW), BF),
            pltpu.VMEM((GW, WIDE), F32),
            pltpu.VMEM((TOK, D), BF),
            pltpu.VMEM((TOK, D), BF),
            pltpu.SemaphoreType.DMA((12,)),
            pltpu.SemaphoreType.DMA((8,)),
            pltpu.SemaphoreType.DMA((8,)),
            pltpu.SemaphoreType.DMA((9,)),
            pltpu.SemaphoreType.DMA((9,)),
            pltpu.SemaphoreType.DMA((11,)),
            pltpu.SemaphoreType.DMA((11,)),
            pltpu.SemaphoreType.DMA((8,)),
            pltpu.SemaphoreType.DMA((8,)),
            pltpu.SemaphoreType.DMA((16,)),
            pltpu.SemaphoreType.DMA((16,)),
        ],
        compiler_params=pltpu.CompilerParams(
            collective_id=0, has_side_effects=True, vmem_limit_bytes=63 * 1024 * 1024
        ),
    )(
        tokens.transpose(1, 2, 0, 3), mixed_grad.transpose(1, 2, 0, 3), qkv_weight, out_weight,
        norm_gain.reshape(1, D), norm_bias.reshape(1, D),
    )
    return m_out.transpose(2, 0, 1, 3), d_out.transpose(2, 0, 1, 3)


def solution(mesh):
    placed = (
        P(None, "lat", "lon", None),
        P("lon", None),
        P("lon", None),
        P(),
        P(),
        P(None, "lat", "lon", None),
    )
    return jax.shard_map(
        functools.partial(per_device, mesh.shape["lat"], mesh.shape["lon"]),
        mesh=mesh,
        in_specs=placed,
        out_specs=(P(None, "lat", "lon", None), P(None, "lat", "lon", None)),
        check_vma=False,
    )
```

profile of v0, /device:TPU:1, one launch (start us, length us, event | category | flops | bytes accessed | tf_op | source)
XLA Modules:
  0.0 83.6 jit_solution(4558334270104029176)
XLA Ops:
  0.6 79.7 %shard_map.77 = (bf16[12,12,2,1024]{3,2,1,0:T(2,128)(2,1)}, bf16[12,12,2,1024]{3,2,1,0:T(2,128)(2,1)}) custom-call(bf16[12,12,2,1024]{3,2,1,0:T(2,128)(2,1)} %bitcast.6, bf16[12,12,2,1024]{3,2,1,0:T(2,128)(2,1)} %bitcast.7, bf16[32,1536]{1,0:T(8,128)(2,1)} %wq_ref.1, bf16[16,1024]{1,0:T(8,128)(2,1)} %wo_ref.1, f32[1,1024]{1,0:T(1,128)} %bitcast.10, ...), custom_call_target="tpu_custom_call" | custom-call | tf_op jit(solution)/shard_map/pallas_call | solution.py:395
  80.4 0.0 copy-start
  80.4 2.4 %copy.10 = bf16[2,12,12,1024]{3,0,2,1:T(2,128)(2,1)} copy(bf16[2,12,12,1024]{3,0,2,1:T(2,128)(2,1)} %bitcast.9) | data formatting | bytes 1179648
  82.8 0.0 copy-done
  82.8 0.8 copy.11
Async XLA Ops:
  80.4 2.4 %copy-start = (bf16[12,12,2,1024]{3,2,1,0:T(2,128)(2,1)S(1)}, bf16[12,12,2,1024]{3,2,1,0:T(2,128)(2,1)}, u32[]{:S(2)}) copy-start(bf16[12,12,2,1024]{3,2,1,0:T(2,128)(2,1)} %get-tuple-element.5) | copy-start | bytes 1769476
where the time goes:
time: 84.6 us; the launch traced here: 83.6 us
  Pallas kernels  79.7 us (94%)
  local copies, waits for them, and re-layouts  3.25 us (4%)
    pallas_call x1, Pallas kernels, per_device(): pl.pallas_call(functools.partial(kernel, n_lat, n_lon), out_shape=[jax.Sh...  79.7 us
    unnamed x4, local copies, waits for them, and re-layouts  3.25 us

commit v1 on v0

--- a/solution.py
+++ b/solution.py
@@ -82,8 +82,6 @@
     def y_to(way):
         return ((half * ny + lax.rem(y + 1 - 2 * way + ny, ny)) * 2 + core, lon)
 
-    opposite = ((half * ny + lax.rem(y + 2, ny)) * 2 + core, lon)
-
     def line(group, c):
         return lax.rem(y + ny + (0, 2 * c - 1, 1 - 2 * c, 2)[group], ny)
 
@@ -98,7 +96,7 @@
 
     barrier = pltpu.get_barrier_semaphore()
     met = [z_to(e) for e in range(4)]
-    met += [y_to(0), y_to(1), opposite, sib, x_to, x_from, west, north, diag, east, south, far]
+    met += [y_to(0), y_to(1), sib, x_to, x_from, west, north, diag, east, south, far]
     for who in met:
         pl.semaphore_signal(barrier, inc=1, device_id=who, device_id_type=MESH)
     for copy in own:
@@ -134,20 +132,21 @@
         return remote(comb[b].at[core, par, 0], comb[b].at[core, par, slot], zs.at[i], zr.at[i], z_to(e))
 
     def y_copy(wave, k):
+        src, dst = ((0, 1), (0, 2), (1, 3))[k]
         i, buf = wave * 3 + k, comb[wave // 2]
         return remote(
-            buf.at[core, par, slots(wave, 0)], buf.at[core, par, slots(wave, k + 1)], ys.at[i], yr.at[i],
-            (y_to(core), y_to(1 - core), opposite)[k],
+            buf.at[core, par, slots(wave, src)], buf.at[core, par, slots(wave, dst)], ys.at[i], yr.at[i],
+            y_to(1 - core if k == 1 else core),
         )
 
     def x_copy(wave, k, p):
-        ref = comb[wave // 2].at[core, p, slots(wave, k, 1 + 2 * k)]
-        i = wave * 2 + k
+        ref = comb[wave // 2].at[core, p, slots(wave, (0, 1, 3)[k], (1, 2, 1)[k])]
+        i = wave * 3 + k
         return remote(ref, ref, xs.at[i], xr.at[i], x_to)
 
     def x_own(b, p):
         ref = comb[b].at[core, p, 0]
-        return remote(ref, ref, xs.at[6 + b], xr.at[6 + b], x_to)
+        return remote(ref, ref, xs.at[9 + b], xr.at[9 + b], x_to)
 
     def s_copy(wave, other, c):
         ref = comb[wave // 2].at[c, lax.rem(par + other, 2), slots(wave, 0, 4)]
@@ -198,7 +197,7 @@
         b = wave // 2
         for copy in z_copies[1] if b else z_copies[0][2 * wave : 2 * wave + 2]:
             copy.wait_recv()
-        for k in (2, 0, 1):
+        for k in range(2):
             y_copy(wave, k).start()
         x_copy(wave, 0, par).start()
         if wave == 0:
@@ -210,16 +209,21 @@
             x_own(1, par).start()
 
     def from_y(wave):
-        for k in range(3):
-            y_copy(wave, k).wait_recv()
+        y_copy(wave, 0).wait_recv()
+        y_copy(wave, 2).start()
+        y_copy(wave, 1).wait_recv()
         x_copy(wave, 1, par).start()
+
+    def from_y2(wave):
+        y_copy(wave, 2).wait_recv()
+        x_copy(wave, 2, par).start()
         s_copy(wave, 0, core).start()
 
     def from_x(wave):
         if wave != 1:
             x_own(wave // 2, 1 - par).wait_recv()
             s_own(wave // 2, core).start()
-        for k in range(2):
+        for k in range(3):
             x_copy(wave, k, 1 - par).wait_recv()
         s_copy(wave, 1, core).start()
 
@@ -233,8 +237,10 @@
     from_z(0)
     from_y(0)
     from_z(1)
+    from_y2(0)
     from_x(0)
     from_y(1)
+    from_y2(1)
     for copy in in_t[0]:
         copy.wait_recv()
     for copy in local:
@@ -251,6 +257,7 @@
     for n in range(3 * INNER // 256):
         cols = slice(n * 256, n * 256 + 256)
         packed[:, cols] = nn(xw[...], wqf[:, cols]).astype(BF)
+    from_y2(2)
 
     lane_head = lax.broadcasted_iota(jnp.int32, (TOK, GW), 1) // HEAD_DIM
     banned = jnp.where(lat == n_lat - 1, -1e30, 0.0).astype(F32)
@@ -375,9 +382,9 @@
     for wave in range(3):
         for k in range(3):
             y_copy(wave, k).wait_send()
-        for k in range(2):
             x_copy(wave, k, par).wait_send()
-            s_copy(wave, k, core).wait_send()
+        for other in range(2):
+            s_copy(wave, other, core).wait_send()
     for b in range(2):
         x_own(b, par).wait_send()
         s_own(b, core).wait_send()

time: 84.6 us -> 82.6 us (0.976)
  Pallas kernels: 79.7 us -> 77.6 us
    pallas_call x1, Pallas kernels: 79.7 us -> 77.6 us  [per_device(): pl.pallas_call(functools.partial(kernel, n_lat, n_lon), out_shape=[jax.Sh...]
where the time goes in v1:
time: 82.6 us; the launch traced here: 81.5 us
  Pallas kernels  77.6 us (94%)
  local copies, waits for them, and re-layouts  3.25 us (4%)
    pallas_call x1, Pallas kernels, per_device(): pl.pallas_call(functools.partial(kernel, n_lat, n_lon), out_shape=[jax.Sh...  77.6 us
    unnamed x4, local copies, waits for them, and re-layouts  3.25 us

profile of v1, /device:TPU:1, one launch (start us, length us, event | category | flops | bytes accessed | tf_op | source)
XLA Modules:
  0.0 81.5 jit_solution(15919633115241728454)
XLA Ops:
  0.6 77.6 %shard_map.77 = (bf16[12,12,2,1024]{3,2,1,0:T(2,128)(2,1)}, bf16[12,12,2,1024]{3,2,1,0:T(2,128)(2,1)}) custom-call(bf16[12,12,2,1024]{3,2,1,0:T(2,128)(2,1)} %bitcast.6, bf16[12,12,2,1024]{3,2,1,0:T(2,128)(2,1)} %bitcast.7, bf16[32,1536]{1,0:T(8,128)(2,1)} %wq_ref.1, bf16[16,1024]{1,0:T(8,128)(2,1)} %wo_ref.1, f32[1,1024]{1,0:T(1,128)} %bitcast.10, ...), custom_call_target="tpu_custom_call" | custom-call | tf_op jit(solution)/shard_map/pallas_call | solution.py:402
  78.3 0.0 copy-start
  78.3 2.4 %copy.10 = bf16[2,12,12,1024]{3,0,2,1:T(2,128)(2,1)} copy(bf16[2,12,12,1024]{3,0,2,1:T(2,128)(2,1)} %bitcast.9) | data formatting | bytes 1179648
  80.7 0.0 copy-done
  80.7 0.8 copy.11
Async XLA Ops:
  78.3 2.4 %copy-start = (bf16[12,12,2,1024]{3,2,1,0:T(2,128)(2,1)S(1)}, bf16[12,12,2,1024]{3,2,1,0:T(2,128)(2,1)}, u32[]{:S(2)}) copy-start(bf16[12,12,2,1024]{3,2,1,0:T(2,128)(2,1)} %get-tuple-element.5) | copy-start | bytes 1769476
